TPU v7x, 512 devices: a whole 4x4x16 slice. The times are simulated.
512 devices in a mesh: space: 16 (over y, x), member: 32 (over z, core).
Axes of the slice: x: 4, y: 4, z: 16, core: 2. Of those that a mesh axis runs over, the one named last changes fastest.
Arguments:
- state: bfloat16 [256, 8192, 128], P('member', 'space'), may hold values from -6 to 6
- obs_prior: bfloat16 [256, 256, 128], P('member', 'space'), may hold values from -6 to 6
- obs_value: float32 [256, 128], P('space'), may hold values from -6 to 6
- obs_precision: float32 [256, 128], P('space'), may hold values from 0.25 to 4
- block_lists: int32 [2048, 16], P(('space', 'member')), may hold values from 0 to 47, as said below
- list_counts: int32 [2048], P(('space', 'member')), may hold values from 4 to 16, as said below
Outputs:
- analysis: bfloat16 [256, 8192, 128], P('member', 'space')
Inputs may be any that keep to these rules, and one draw needn't show every extreme that they name: `block_lists`: each row names 16 different blocks. `list_counts`: some group uses all 16 entries.
All inputs are finite; a program needn't handle non-finite values.
Results may differ from a plain program's by a relative error of at most 0.0055.
Values may be sent and summed in bfloat16 or wider, within the bound.
A program may use at most 64 MiB of HBM per device.

v0:
```python
import jax
import jax.numpy as jnp
from jax import lax
from jax.sharding import PartitionSpec as P

NS_ITERS = 6


def extended(block, sides, width):
    for axis, dim in sides:
        count = lax.axis_size(axis)
        forward = [(i, i + 1) for i in range(count - 1)]
        backward = [(target, source) for source, target in forward]
        low = lax.ppermute(
            lax.slice_in_dim(block, block.shape[dim] - width, None, axis=dim), axis, forward
        )
        high = lax.ppermute(lax.slice_in_dim(block, 0, width, axis=dim), axis, backward)
        block = jnp.concatenate([low, block, high], axis=dim)
    return block


def newton_schulz(system):
    size = system.shape[0]
    identity = jnp.eye(size, dtype=jnp.float32)
    frob_norm = jnp.sqrt(jnp.sum(system * system))
    iterate = system / frob_norm
    inverse_half = identity
    for sweep in range(NS_ITERS):
        factor = 1.5 * identity - 0.5 * jnp.dot(
            inverse_half, iterate, precision=lax.Precision.HIGHEST
        )
        iterate = jnp.dot(iterate, factor, precision=lax.Precision.HIGHEST)
        inverse_half = jnp.dot(factor, inverse_half, precision=lax.Precision.HIGHEST)
    return (inverse_half, frob_norm)


def solve_weights(picked, precision_rows, innovation_rows):
    members = picked.shape[0]
    matrix = picked.reshape(members, -1)
    weight_flat = precision_rows.reshape(-1)
    scaled = (matrix.astype(jnp.float32) * weight_flat).astype(jnp.bfloat16)
    product = lax.dot_general(
        matrix, scaled, (((1,), (1,)), ((), ())), preferred_element_type=jnp.float32
    )
    system = (members - 1.0) * jnp.eye(members, dtype=jnp.float32) + product
    weighted_innov = (weight_flat * innovation_rows.reshape(-1)).astype(jnp.bfloat16)
    forcing = jnp.dot(matrix, weighted_innov, preferred_element_type=jnp.float32)
    inverse_half, frob_norm = newton_schulz(system)
    inverse_full = jnp.dot(inverse_half, inverse_half, precision=lax.Precision.HIGHEST) / frob_norm
    weight_mean = jnp.dot(inverse_full, forcing, precision=lax.Precision.HIGHEST)
    return jnp.sqrt(members - 1.0) * inverse_half / jnp.sqrt(frob_norm) + weight_mean[:, None]


def apply_weights(xblock, weights):
    members = xblock.shape[0]
    matrix = xblock.reshape(members, -1).astype(jnp.float32)
    average = jnp.mean(matrix, axis=0)
    departure = matrix - average
    updated = average + lax.dot_general(
        weights, departure, (((0,), (0,)), ((), ())), precision=lax.Precision.HIGHEST
    )
    return updated.astype(jnp.bfloat16).reshape(xblock.shape)


def per_device(state, obs_prior, obs_value, obs_precision, block_lists, list_counts):
    rim_width = obs_prior.shape[1]
    own_tile = lax.all_gather(obs_prior, "member", axis=0, tiled=True)
    gathered = extended(own_tile, (("space", 1),), rim_width)
    values_rim, precision_rim = (
        extended(obs_value, (("space", 0),), rim_width),
        extended(obs_precision, (("space", 0),), rim_width),
    )
    prior32 = gathered.astype(jnp.float32)
    prior_mean = jnp.mean(prior32, axis=0)
    anomaly = (prior32 - prior_mean).astype(jnp.bfloat16)
    innovation = values_rim - prior_mean
    columns = lax.all_to_all(state, "member", split_axis=1, concat_axis=0, tiled=True)
    group_count = block_lists.shape[0]
    list_length = block_lists.shape[1]

    def solve(group):
        chosen = block_lists[group]
        picked = jnp.take(anomaly, chosen, axis=1)
        active = (jnp.arange(list_length, dtype=jnp.int32) < list_counts[group]).astype(jnp.float32)
        precision_rows = jnp.take(precision_rim, chosen, axis=0) * active[:, None]
        innovation_rows = jnp.take(innovation, chosen, axis=0)
        weights = solve_weights(picked, precision_rows, innovation_rows)
        xblock = lax.dynamic_slice_in_dim(columns, group * 4, 4, 1)
        return apply_weights(xblock, weights)

    numbers = jnp.arange(group_count, dtype=jnp.int32)
    result = lax.map(solve, numbers)
    members = columns.shape[0]
    merged = jnp.transpose(result, (1, 0, 2, 3)).reshape(members, group_count * 4, columns.shape[2])
    return lax.all_to_all(merged, "member", split_axis=0, concat_axis=1, tiled=True)


def solution(mesh):
    in_specs = (
        P("member", "space", None),
        P("member", "space", None),
        P("space", None),
        P("space", None),
        P(("space", "member"), None),
        P(("space", "member")),
    )
    out_specs = P("member", "space", None)
    return jax.shard_map(
        per_device, mesh=mesh, in_specs=in_specs, out_specs=out_specs, check_vma=False
    )
```

profile of v0, /device:TPU:1, one launch (start us, length us, event | category | flops | bytes accessed | tf_op | source)
XLA Modules:
  0.0 300.5 jit_solution(2678140305268309568)
XLA Ops:
  6.5 2.9 copy.19
  9.5 16.7 %all-to-all-start = ((bf16[8,512,128]{2,0,1:T(8,128)(2,1)}), bf16[8,512,128]{2,0,1:T(8,128)(2,1)S(1)}, u32[]{:S(2)}, u32[]{:S(2)}) async-start(bf16[8,512,128]{2,0,1:T(8,128)(2,1)} %copy.19), calls=%async_computation | async-start | bytes 2097152 | tf_op jit(solution)/shard_map/all_to_all | solution.py:77
  26.9 85.3 %all-gather.2.cloned.1.call-done = bf16[256,16,128]{2,0,1:T(8,128)(2,1)} async-done(((bf16[8,16,128]{2,0,1:T(8,128)(2,1)}), bf16[256,16,128]{2,0,1:T(8,128)(2,1)}) %all-gather.2.cloned.1.call-update) | async-done | bytes 1048592 | tf_op jit(solution)/shard_map/all_gather | solution.py:67
  112.2 3.3 %collective-permute-start = (bf16[256,16,128]{2,0,1:T(8,128)(2,1)}, bf16[256,16,128]{2,0,1:T(8,128)(2,1)S(1)}, u32[]{:S(2)}, u32[]{:S(2)}) collective-permute-start(bf16[256,16,128]{2,0,1:T(8,128)(2,1)} %all-gather.2.cloned.1.call-done), channel_id=1, source_target_pairs={{0,32},{32,64},{64,96},{96,128},{128,160},{160,192},{192,224},{224... | collective-permute-start | bytes 3145736 | tf_op jit(solution)/shard_map/ppermute | solution.py:14
  115.5 1.3 collective-permute-start.1
  116.8 4.0 %collective-permute-start.2 = (f32[16,128]{1,0:T(8,128)S(1)}, f32[16,128]{1,0:T(8,128)S(1)}, u32[]{:S(2)}, u32[]{:S(2)}) collective-permute-start(f32[16,128]{1,0:T(8,128)S(1)} %copy-done.3), channel_id=1, source_target_pairs={{0,32},{32,64},{64,96},{96,128},{128,160},{160,192},{192,224},{224... | collective-permute-start | bytes 24584 | tf_op jit(solution)/shard_map/ppermute | solution.py:14
  120.8 1.3 collective-permute-start.3
  122.1 4.0 %collective-permute-start.4 = (f32[16,128]{1,0:T(8,128)S(1)}, f32[16,128]{1,0:T(8,128)S(1)}, u32[]{:S(2)}, u32[]{:S(2)}) collective-permute-start(f32[16,128]{1,0:T(8,128)S(1)} %copy-done.2), channel_id=1, source_target_pairs={{0,32},{32,64},{64,96},{96,128},{128,160},{160,192},{192,224},{224... | collective-permute-start | bytes 24584 | tf_op jit(solution)/shard_map/ppermute | solution.py:14
  126.1 12.0 %collective-permute-done.2 = f32[16,128]{1,0:T(8,128)S(1)} collective-permute-done((f32[16,128]{1,0:T(8,128)S(1)}, f32[16,128]{1,0:T(8,128)S(1)}, u32[]{:S(2)}, u32[]{:S(2)}) %collective-permute-start.2) | collective-permute-done | bytes 8224 | tf_op jit(solution)/shard_map/ppermute | solution.py:14
  138.1 1.3 collective-permute-start.5
  139.4 2.7 collective-permute-done.3
  142.1 1.9 convert_reduce_fusion
  144.0 3.4 %fusion.31 = bf16[256,48,128]{2,0,1:T(8,128)(2,1)} fusion(f32[48,128]{1,0:T(8,128)S(1)} %get-tuple-element.80, bf16[256,16,128]{2,0,1:T(8,128)(2,1)} %collective-permute-done.1, bf16[256,16,128]{2,0,1:T(8,128)(2,1)S(1)} %copy-done, bf16[256,16,128]{2,0,1:T(8,128)(2,1)S(1)} %collective-permute-done), kind=kLoop, calls=%fused_computation.63 | loop fusion | flops 7864320 | bytes 6316032 | tf_op jit(solution)/shard_map/convert_element_type | solution.py:75
  147.7 78.9 %while.10 = (s32[]{:T(128)}, bf16[4,256,4,128]{3,1,2,0:T(8,128)(2,1)}, s32[4]{0:T(128)S(1)}, bf16[256,16,128]{2,1,0:T(8,128)(2,1)S(1)}, s32[4,16]{1,0:T(4,128)S(...) while((s32[]{:T(128)}, ...), condition=%wide.region_4.6_spmd, body=%wide.region_1.5_spmd.sunk | while | flops 4303171584 | bytes 21329436 | solution.py:92
  152.7 2.6 gather_fusion.2
  155.3 1.2 multiply_reduce_fusion.2
  165.9 0.7 fusion.193
  166.7 0.7 copy_dynamic-update-slice_fusion.2
  172.4 2.6 gather_fusion.2
  175.0 1.2 multiply_reduce_fusion.2
  185.6 0.7 fusion.193
  186.4 0.7 copy_dynamic-update-slice_fusion.2
  192.1 2.6 gather_fusion.2
  194.8 1.2 multiply_reduce_fusion.2
  205.3 0.7 fusion.193
  206.1 0.7 copy_dynamic-update-slice_fusion.2
  211.8 2.6 gather_fusion.2
  214.5 1.2 multiply_reduce_fusion.2
  225.8 0.7 copy_dynamic-update-slice_fusion.2
  226.6 1.9 copy.23
  228.5 64.0 %all_to_all.36 = bf16[256,16,128]{2,1,0:T(8,128)(2,1)S(1)} all-to-all(bf16[256,16,128]{2,1,0:T(8,128)(2,1)S(1)} %copy.23), channel_id=1, replica_groups=mesh['space'=16,'member'=32] {'member'}, dimensions={0} | all-to-all | bytes 2097152 | tf_op jit(solution)/shard_map/all_to_all | solution.py:95
  292.5 1.2 copy.24
  (158 shorter events, 45.5 us)
Async XLA Ops:
  6.5 19.7 %copy-start.1 = (bf16[8,16,128]{2,1,0:T(8,128)(2,1)S(1)}, bf16[8,16,128]{2,1,0:T(8,128)(2,1)}, u32[]{:S(2)}) copy-start(bf16[8,16,128]{2,1,0:T(8,128)(2,1)} %param.11) | copy-start | bytes 98308
  6.5 110.3 %copy-start.3 = (f32[16,128]{1,0:T(8,128)S(1)}, f32[16,128]{1,0:T(8,128)}, u32[]{:S(2)}) copy-start(f32[16,128]{1,0:T(8,128)} %param.13) | copy-start | bytes 24580
  6.5 115.6 %copy-start.2 = (f32[16,128]{1,0:T(8,128)S(1)}, f32[16,128]{1,0:T(8,128)}, u32[]{:S(2)}) copy-start(f32[16,128]{1,0:T(8,128)} %param.12) | copy-start | bytes 24580
  9.5 138.0 %all-to-all-start = ((bf16[8,512,128]{2,0,1:T(8,128)(2,1)}), bf16[8,512,128]{2,0,1:T(8,128)(2,1)S(1)}, u32[]{:S(2)}, u32[]{:S(2)}) async-start(bf16[8,512,128]{2,0,1:T(8,128)(2,1)} %copy.19), calls=%async_computation | async-start | bytes 2097152 | tf_op jit(solution)/shard_map/all_to_all | solution.py:77
  26.2 86.0 %all-gather.2.cloned.1.call-start = ((), (), s32[]{:S(2)}) async-start(), calls=%async_computation.2 | async-start | bytes 1081344 | tf_op jit(solution)/shard_map/all_gather | solution.py:67
  112.2 31.8 %copy-start = (bf16[256,16,128]{2,0,1:T(8,128)(2,1)S(1)}, bf16[256,16,128]{2,0,1:T(8,128)(2,1)}, u32[]{:S(2)}) copy-start(bf16[256,16,128]{2,0,1:T(8,128)(2,1)} %all-gather.2.cloned.1.call-done) | copy-start | bytes 3145732
  112.2 29.8 %collective-permute-start = (bf16[256,16,128]{2,0,1:T(8,128)(2,1)}, bf16[256,16,128]{2,0,1:T(8,128)(2,1)S(1)}, u32[]{:S(2)}, u32[]{:S(2)}) collective-permute-start(bf16[256,16,128]{2,0,1:T(8,128)(2,1)} %all-gather.2.cloned.1.call-done), channel_id=1, source_target_pairs={{0,32},{32,64},{64,96},{96,128},{128,160},{160,192},{192,224},{224... | collective-permute-start | bytes 3145736 | tf_op jit(solution)/shard_map/ppermute | solution.py:14
  115.5 26.6 %collective-permute-start.1 = (bf16[256,16,128]{2,0,1:T(8,128)(2,1)}, bf16[256,16,128]{2,0,1:T(8,128)(2,1)}, u32[]{:S(2)}, u32[]{:S(2)}) collective-permute-start(bf16[256,16,128]{2,0,1:T(8,128)(2,1)} %all-gather.2.cloned.1.call-done), channel_id=1, source_target_pairs={{32,0},{64,32},{96,64},{128,96},{160,128},{192,160},{224,192},{256... | collective-permute-start | bytes 3145736 | tf_op jit(solution)/shard_map/ppermute | solution.py:17
  116.8 21.3 %collective-permute-start.2 = (f32[16,128]{1,0:T(8,128)S(1)}, f32[16,128]{1,0:T(8,128)S(1)}, u32[]{:S(2)}, u32[]{:S(2)}) collective-permute-start(f32[16,128]{1,0:T(8,128)S(1)} %copy-done.3), channel_id=1, source_target_pairs={{0,32},{32,64},{64,96},{96,128},{128,160},{160,192},{192,224},{224... | collective-permute-start | bytes 24584 | tf_op jit(solution)/shard_map/ppermute | solution.py:14
  120.8 21.2 %collective-permute-start.3 = (f32[16,128]{1,0:T(8,128)S(1)}, f32[16,128]{1,0:T(8,128)S(1)}, u32[]{:S(2)}, u32[]{:S(2)}) collective-permute-start(f32[16,128]{1,0:T(8,128)S(1)} %copy-done.3), channel_id=1, source_target_pairs={{32,0},{64,32},{96,64},{128,96},{160,128},{192,160},{224,192},{256... | collective-permute-start | bytes 24584 | tf_op jit(solution)/shard_map/ppermute | solution.py:17
  122.1 21.8 %collective-permute-start.4 = (f32[16,128]{1,0:T(8,128)S(1)}, f32[16,128]{1,0:T(8,128)S(1)}, u32[]{:S(2)}, u32[]{:S(2)}) collective-permute-start(f32[16,128]{1,0:T(8,128)S(1)} %copy-done.2), channel_id=1, source_target_pairs={{0,32},{32,64},{64,96},{96,128},{128,160},{160,192},{192,224},{224... | collective-permute-start | bytes 24584 | tf_op jit(solution)/shard_map/ppermute | solution.py:14
  138.1 5.9 %collective-permute-start.5 = (f32[16,128]{1,0:T(8,128)S(1)}, f32[16,128]{1,0:T(8,128)S(1)}, u32[]{:S(2)}, u32[]{:S(2)}) collective-permute-start(f32[16,128]{1,0:T(8,128)S(1)} %copy-done.2), channel_id=1, source_target_pairs={{32,0},{64,32},{96,64},{128,96},{160,128},{192,160},{224,192},{256... | collective-permute-start | bytes 24584 | tf_op jit(solution)/shard_map/ppermute | solution.py:17
  144.0 3.7 %copy-start.4 = (s32[4,16]{1,0:T(4,128)S(1)}, s32[4,16]{1,0:T(4,128)}, u32[]{:S(2)}) copy-start(s32[4,16]{1,0:T(4,128)} %param.14) | copy-start | bytes 772
  144.0 3.7 %copy-start.5 = (s32[4]{0:T(128)S(1)}, s32[4]{0:T(128)}, u32[]{:S(2)}) copy-start(s32[4]{0:T(128)} %param.15) | copy-start | bytes 52
Sparse Core Ops, SparseCore 0:
  29.1 83.0 all-gather.1
where the time goes:
time: 303 us; the launch traced here: 300 us
  waiting for transfers between devices  100 us (33%)
  blocking collectives  64 us (21%)
  matrix products  37.3 us (12%)
  starting transfers between devices  31.9 us (11%)
  local copies, waits for them, and re-layouts  30.1 us (10%)
  loops' own time  13.9 us (5%)
  between operations  13.6 us (4%)
  other arithmetic  9.81 us (3%)
    all_gather x1, waiting for transfers between devices, per_device(): own_tile = lax.all_gather(obs_prior, 'member', axis=0, tiled=True)  85.3 us
    all_to_all x1, blocking collectives, per_device(): lax.all_to_all(merged, 'member', split_axis=0, concat_axis=1, tiled=True)  64 us
    all_to_all x1, starting transfers between devices, per_device(): lax.all_to_all(state, 'member', split_axis=1, concat_axis=0, tiled=True)  16.7 us
    another operation x1, loops' own time, per_device(): result = lax.map(solve, numbers)  13.9 us
    ppermute x3, waiting for transfers between devices, extended(): lax.ppermute(lax.slice_in_dim(block, block.shape[dim] - width, None, axis...  12 us
    ppermute x3, starting transfers between devices, extended(): lax.ppermute(lax.slice_in_dim(block, block.shape[dim] - width, None, axis...  11.3 us
    gather x4, local copies, waits for them, and re-layouts, solve(): picked = jnp.take(anomaly, chosen, axis=1)  10.6 us
    dot_general x24, matrix products, newton_schulz(): jnp.dot(inverse_half, iterate, precision=lax.Precision.HIGHEST)  8.88 us
  transfers between devices with their start and end apart: 8, of which 3 were waited for; matrix products, arithmetic and copies ran while one was open for 2% of the time, Pallas kernels for 0%

commit v1 on v0

v1 whole, which is shorter than its diff:
```python
import math

import jax
import jax.numpy as jnp
from jax import lax
from jax.experimental import pallas as pl
from jax.experimental.pallas import tpu as pltpu
from jax.sharding import PartitionSpec as P

MESH = pl.DeviceIdType.MESH
BF, F32 = jnp.bfloat16, jnp.float32
NS_ITERS = 6
NG = 4
MEM = 256
NZ = 16
NSP = 16


def split(x):
    high = x.astype(BF)
    return high, (x - high.astype(F32)).astype(BF)


def dot(a, b):
    return lax.dot_general(a, b, (((1,), (0,)), ((), ())), preferred_element_type=F32)


def dot3(a, b):
    (ah, al), (bh, bl) = a, b
    return dot(jnp.concatenate([ah, al, ah], 1), jnp.concatenate([bh, bh, bl], 0))


def eye():
    rows = lax.broadcasted_iota(jnp.int32, (MEM, MEM), 0)
    return (rows == lax.broadcasted_iota(jnp.int32, (MEM, MEM), 1)).astype(F32)


def loop(low, high, body):
    def step(i, carry):
        body(i)
        return carry

    lax.fori_loop(low, high, step, 0)


def anomalies(s, raw, vp, stage, anom, prec, inno):
    for tile in range(3):
        def add(slot, total):
            return total + jnp.sum(raw[tile, slot].astype(F32), axis=0)

        mean = lax.fori_loop(0, 32, add, jnp.zeros((16, 128), F32)) * (1.0 / MEM)
        live = jnp.float32(1.0)
        if tile == 0:
            live = jnp.where(s > 0, 1.0, 0.0).astype(F32)
        if tile == 2:
            live = jnp.where(s < NSP - 1, 1.0, 0.0).astype(F32)

        def centre(slot):
            rows = (raw[tile, slot].astype(F32) - mean[None]) * live
            stage[pl.ds(pl.multiple_of(slot * 128, 128), 128), :] = rows.reshape(128, 128)

        loop(0, 32, centre)

        def pick(b):
            anom[tile * 16 + b] = stage[pl.ds(b, MEM, stride=16), :].astype(BF)

        loop(0, 16, pick)
        innovation = (vp[tile, 0] - mean) * live
        precision = vp[tile, 1] * live
        for b in range(16):
            inno[tile * 16 + b] = innovation[b : b + 1]
            prec[tile * 16 + b] = precision[b : b + 1]


def systems(lists, counts, anom, prec, inno, t_ref, f_ref):
    def group(g):
        count = counts[g]
        total = jnp.zeros((MEM + 16, MEM), F32)
        for pair in range(8):
            ys, ss, ws = [], [], []
            for e in (2 * pair, 2 * pair + 1):
                b = lists[g, e]
                y = anom[b]
                r = prec[b] * jnp.where(e < count, 1.0, 0.0).astype(F32)
                ys.append(y)
                ss.append((y.astype(F32) * r).astype(BF))
                ws.append(jnp.broadcast_to((r * inno[b]).astype(BF), (16, 128)))
            left = jnp.concatenate([jnp.concatenate(ss, 1), jnp.concatenate(ws, 1)], 0)
            total = total + lax.dot_general(
                left, jnp.concatenate(ys, 1), (((1,), (1,)), ((), ())), preferred_element_type=F32
            )
        t_ref[g] = total[:MEM] + (MEM - 1.0) * eye()
        f_ref[g] = total[MEM:]

    loop(0, NG, group)


def weights(t_ref, f_ref, p_ref, z_ref, w_ref):
    def first(g):
        t = t_ref[g]
        norm = jnp.sqrt(jnp.sum(t * t, keepdims=True))
        iterate = t / norm
        factor = split(1.5 * eye() - 0.5 * iterate)
        z_ref[g, 0], z_ref[g, 1] = factor
        p_ref[g, 0], p_ref[g, 1] = split(dot3(split(iterate), factor))
        t_ref[g, 0:8, 0:128] = jnp.broadcast_to(norm, (8, 128))

    loop(0, NG, first)

    def sweep(step):
        g = lax.rem(step, NG)
        z = z_ref[g, 0], z_ref[g, 1]
        p = p_ref[g, 0], p_ref[g, 1]
        factor = split(1.5 * eye() - 0.5 * dot3(z, p))
        p_ref[g, 0], p_ref[g, 1] = split(dot3(p, factor))
        z_ref[g, 0], z_ref[g, 1] = split(dot3(factor, z))

    loop(0, (NS_ITERS - 1) * NG, sweep)

    def last(g):
        z = z_ref[g, 0], z_ref[g, 1]
        norm = t_ref[g, 0:1, 0:1]
        mean = dot3(split(dot3(split(f_ref[g]), z)), z)[0:1] / norm
        w = (z[0].astype(F32) + z[1].astype(F32)) * (math.sqrt(MEM - 1.0) / jnp.sqrt(norm)) + mean
        w = w + (1.0 - jnp.sum(w, axis=1, keepdims=True)) * (1.0 / MEM)
        w_ref[g, 0], w_ref[g, 1] = split(w)

    loop(0, NG, last)


def kernel(
    lists, counts, state, obs, value, precision, out,
    raw, vp, stage, anom, prec, inno, t_ref, f_ref, p_ref, z_ref, w_ref, cols, xb, stage2, outb,
    rps, rpr, rms, rmr, sbs, sbr, has, har, shs, shr, vps, vpr, s1, r1, s2, r2, own,
):
    s, me = lax.axis_index("space"), lax.axis_index("member")
    z, c = me // 2, me % 2
    zp, zm = ((z + 1) % NZ) * 2 + c, ((z + NZ - 1) % NZ) * 2 + c
    sibling = z * 2 + 1 - c
    up, down = (s + 1) % NSP, (s + NSP - 1) % NSP

    barrier = pltpu.get_barrier_semaphore()
    for peer in (up, down):
        pl.semaphore_signal(barrier, inc=1, device_id=(peer, me), device_id_type=MESH)

    def greet(d):
        pl.semaphore_signal(barrier, inc=1, device_id=(s, (me + d) % 32), device_id_type=MESH)

    loop(1, 32, greet)
    pl.semaphore_wait(barrier, 33)

    def rcopy(src, dst, ss, rs, device):
        return pltpu.make_async_remote_copy(
            src_ref=src, dst_ref=dst, send_sem=ss, recv_sem=rs, device_id=device, device_id_type=MESH
        )

    def ring_up(t):
        return rcopy(raw.at[1, 2 * ((16 - t) % 16)], raw.at[1, 2 * (15 - t)], rps.at[t], rpr.at[t], (s, zp))

    def ring_down(t):
        return rcopy(raw.at[1, 2 * t], raw.at[1, 2 * (t + 1)], rms.at[t], rmr.at[t], (s, zm))

    def across(u):
        return rcopy(raw.at[1, 2 * u], raw.at[1, 2 * u + 1], sbs.at[u], sbr.at[u], (s, sibling))

    def halo(side, u):
        dst = raw.at[2 * side, 2 * u]
        return rcopy(raw.at[1, 2 * u], dst, has.at[side, u], har.at[side, u], ((up, down)[side], me))

    def halo_across(side, u):
        tile = 2 * side
        return rcopy(
            raw.at[tile, 2 * u], raw.at[tile, 2 * u + 1], shs.at[side, u], shr.at[side, u], (s, sibling)
        )

    def rim(side):
        return rcopy(vp.at[1], vp.at[2 * side], vps.at[side], vpr.at[side], ((up, down)[side], me))

    def far(j):
        return (8 + ((j + 1) // 2) * (2 * ((j + 1) % 2) - 1)) % 16

    def place(u, p):
        core = c if p == 0 else 1 - c
        return 2 * ((z + u) % NZ) + core

    def rows_of(member):
        return pl.ds(pl.multiple_of(member * 16, 16), 16)

    def send_state(u, p):
        target = place(u, p)
        slot = 2 * ((16 - u) % 16) + p
        return rcopy(
            state.at[:, rows_of(target), :], cols.at[slot], s1.at[2 * u + p], r1.at[slot], (s, target)
        )

    def send_result(u, p):
        target = place(u, p)
        slot = 2 * ((16 - u) % 16) + p
        return rcopy(
            outb.at[2 * u + p], out.at[:, rows_of(me), :], s2.at[2 * u + p], r2.at[slot], (s, target)
        )

    def spread(u):
        across(u).start()
        halo(0, u).start()
        halo(1, u).start()

    def relay(u):
        for side in range(2):
            halo(side, u).wait_recv()
            halo_across(side, u).start()

    own_in = pltpu.make_async_copy(state.at[:, rows_of(me), :], cols.at[0], own.at[0])
    own_in.start()
    raw[1, 0] = obs[...]
    vp[1, 0] = value[...]
    vp[1, 1] = precision[...]
    ring_up(0).start()
    ring_down(0).start()
    spread(0)
    rim(0).start()
    rim(1).start()

    def scatter(j):
        u = far(j)
        send_state(u, 0).start()
        send_state(u, 1).start()

    scatter(0)
    scatter(1)

    def step(t):
        ring_up(t - 1).wait_recv()
        ring_up(t).start()
        ring_down(t - 1).wait_recv()

        @pl.when(t < 7)
        def _():
            ring_down(t).start()

        spread(16 - t)
        spread(t)

        @pl.when(t > 1)
        def _():
            relay(17 - t)
            relay(t - 1)

        scatter(2 * t)

        @pl.when(t < 7)
        def _():
            scatter(2 * t + 1)

    loop(1, 8, step)
    send_state(0, 1).start()
    ring_up(7).wait_recv()
    spread(8)
    relay(0)
    relay(9)
    relay(7)
    relay(8)

    def landed(u):
        across(u).wait_recv()
        halo_across(0, u).wait_recv()
        halo_across(1, u).wait_recv()

    loop(0, 16, landed)
    rim(0).wait_recv()
    rim(1).wait_recv()

    anomalies(s, raw, vp, stage, anom, prec, inno)
    systems(lists, counts, anom, prec, inno, t_ref, f_ref)
    weights(t_ref, f_ref, p_ref, z_ref, w_ref)

    def unpack(slot):
        rows = cols[slot].astype(F32).reshape(128, 128)
        stage[pl.ds(pl.multiple_of(slot * 128, 128), 128), :] = rows

    own_in.wait()
    unpack(0)

    def arrive(slot):
        rcopy(
            state.at[:, pl.ds(0, 16), :], cols.at[slot], s1.at[slot], r1.at[slot], (s, sibling)
        ).wait_recv()
        unpack(slot)

    loop(1, 32, arrive)
    for g in range(NG):
        for r in range(4):
            xb[g, :, r * 128 : (r + 1) * 128] = stage[pl.ds(4 * g + r, MEM, stride=16), :].astype(BF)

    def apply(part):
        far_of = [far(4 * part + i) for i in range(4)]
        for g in range(NG):
            left = [
                w_ref[g, h, pl.ds(pl.multiple_of(u * 16, 16), 16), :] for h in range(2) for u in far_of
            ]
            both = dot(jnp.concatenate(left, 0), xb[g])
            done = both[:64] + both[64:]
            for r in range(4):
                stage2[pl.ds(4 * g + r, 64, stride=16), :] = done[:, r * 128 : (r + 1) * 128]
        for i, u in enumerate(far_of):
            for p in range(2):
                rows = stage2[pl.ds((2 * i + p) * 128, 128), :]
                outb[2 * u + p] = rows.reshape(8, 16, 128).astype(BF)
                if i == 3 and p == 0:

                    @pl.when(part < 3)
                    def _():
                        send_result(u, p).start()
                else:
                    send_result(u, p).start()

    loop(0, 4, apply)
    own_out = pltpu.make_async_copy(outb.at[0], out.at[:, rows_of(me), :], own.at[1])
    own_out.start()

    def settle(slot):
        rcopy(
            outb.at[slot], out.at[:, pl.ds(0, 16), :], s2.at[slot], r2.at[slot], (s, sibling)
        ).wait()
        rcopy(
            state.at[:, pl.ds(0, 16), :], cols.at[slot], s1.at[slot], r1.at[slot], (s, sibling)
        ).wait_send()

    loop(1, 32, settle)
    own_out.wait()

    def sent(t):
        ring_up(t).wait_send()

        @pl.when(t < 7)
        def _():
            ring_down(t).wait_send()

    loop(0, 8, sent)

    def sent_wide(u):
        across(u).wait_send()
        for side in range(2):
            halo(side, u).wait_send()
            halo_across(side, u).wait_send()

    loop(0, 16, sent_wide)
    rim(0).wait_send()
    rim(1).wait_send()


def per_device(state, obs_prior, obs_value, obs_precision, block_lists, list_counts):
    vmem = pl.BlockSpec(memory_space=pltpu.VMEM)
    smem = pl.BlockSpec(memory_space=pltpu.SMEM)
    anywhere = pl.BlockSpec(memory_space=pl.ANY)
    dma = pltpu.SemaphoreType.DMA
    return pl.pallas_call(
        kernel,
        out_shape=jax.ShapeDtypeStruct(state.shape, state.dtype),
        in_specs=[smem, smem, anywhere, vmem, vmem, vmem],
        out_specs=anywhere,
        scratch_shapes=[
            pltpu.VMEM((3, 32, 8, 16, 128), BF),
            pltpu.VMEM((3, 2, 16, 128), F32),
            pltpu.VMEM((4096, 128), F32),
            pltpu.VMEM((48, MEM, 128), BF),
            pltpu.VMEM((48, 1, 128), F32),
            pltpu.VMEM((48, 1, 128), F32),
            pltpu.VMEM((NG, MEM, MEM), F32),
            pltpu.VMEM((NG, 16, MEM), F32),
            pltpu.VMEM((NG, 2, MEM, MEM), BF),
            pltpu.VMEM((NG, 2, MEM, MEM), BF),
            pltpu.VMEM((NG, 2, MEM, MEM), BF),
            pltpu.VMEM((32, 8, 16, 128), BF),
            pltpu.VMEM((NG, MEM, 512), BF),
            pltpu.VMEM((1024, 128), F32),
            pltpu.VMEM((32, 8, 16, 128), BF),
            dma((8,)), dma((8,)), dma((7,)), dma((7,)), dma((16,)), dma((16,)),
            dma((2, 16)), dma((2, 16)), dma((2, 16)), dma((2, 16)), dma((2,)), dma((2,)),
            dma((32,)), dma((32,)), dma((32,)), dma((32,)), dma((2,)),
        ],
        compiler_params=pltpu.CompilerParams(
            collective_id=0, has_side_effects=True, vmem_limit_bytes=48 << 20
        ),
        name="analysis",
    )(block_lists, list_counts, state, obs_prior, obs_value, obs_precision)


def solution(mesh):
    in_specs = (
        P("member", "space", None),
        P("member", "space", None),
        P("space", None),
        P("space", None),
        P(("space", "member"), None),
        P(("space", "member")),
    )
    out_specs = P("member", "space", None)
    return jax.shard_map(
        per_device, mesh=mesh, in_specs=in_specs, out_specs=out_specs, check_vma=False
    )
```

time: 303 us -> 160 us (0.53)
  Pallas kernels: 0 us -> 154 us
  waiting for transfers between devices: 100 us -> 0 us
  blocking collectives: 64 us -> 0 us
  matrix products: 37.3 us -> 0 us
  starting transfers between devices: 31.9 us -> 0 us
  local copies, waits for them, and re-layouts: 30.1 us -> 5.68 us
  loops' own time: 13.9 us -> 0 us
  between operations: 13.6 us -> 0.02 us
  other arithmetic: 9.81 us -> 0 us
    pallas_call x0 -> x1, Pallas kernels: none -> 154 us  [per_device(): pl.pallas_call(kernel, out_shape=jax.ShapeDtypeStruct(state.shape, state....]
    all_gather x1 -> x0, waiting for transfers between devices: 85.3 us -> none  [per_device(): own_tile = lax.all_gather(obs_prior, 'member', axis=0, tiled=True)]
    all_to_all x1 -> x0, blocking collectives: 64 us -> none  [per_device(): lax.all_to_all(merged, 'member', split_axis=0, concat_axis=1, tiled=True)]
    dot_general x88 -> x0, matrix products: 37.3 us -> none  [the longest x24 8.88 us: newton_schulz(): jnp.dot(inverse_half, iterate, precision=lax.Precision.HIGHEST)]
    all_to_all x1 -> x0, starting transfers between devices: 16.7 us -> none  [per_device(): lax.all_to_all(state, 'member', split_axis=1, concat_axis=0, tiled=True)]
    ppermute x6 -> x0, starting transfers between devices: 15.1 us -> none  [the longest x3 11.3 us: extended(): lax.ppermute(lax.slice_in_dim(block, block.shape[dim] - width, None, axis...]
    gather x12 -> x0, local copies, waits for them, and re-layouts: 15 us -> none  [the longest x4 10.6 us: solve(): picked = jnp.take(anomaly, chosen, axis=1)]
    ppermute x6 -> x0, waiting for transfers between devices: 14.6 us -> none  [the longest x3 12 us: extended(): lax.ppermute(lax.slice_in_dim(block, block.shape[dim] - width, None, axis...]
  transfers between devices with their start and end apart: 8 -> 0, of which waited for: 3 -> 0; matrix products, arithmetic and copies ran while one was open for 2% -> 0% of each run, Pallas kernels for 0% -> 0%
where the time goes in v1:
time: 160 us
  Pallas kernels  154 us (96%)
  local copies, waits for them, and re-layouts  5.68 us (4%)
    pallas_call x1, Pallas kernels, per_device(): pl.pallas_call(kernel, out_shape=jax.ShapeDtypeStruct(state.shape, state....  154 us
    unnamed x13, local copies, waits for them, and re-layouts  5.68 us

profile of v1, /device:TPU:1, one launch (start us, length us, event | category | flops | bytes accessed | tf_op | source)
XLA Modules:
  0.0 160.2 jit_solution(5203895865065830296)
XLA Ops:
  0.0 0.0 copy-start
  0.0 1.2 copy-done
  1.2 0.0 copy-start.1
  1.2 0.8 copy-done.1
  2.0 0.0 copy-start.2
  2.0 0.7 copy-done.2
  2.7 0.0 copy-start.3
  2.7 0.7 copy-done.3
  3.4 0.0 copy-start.4
  3.4 0.7 copy-done.4
  4.1 0.0 copy-start.5
  4.1 0.7 copy-done.5
  4.7 154.5 %analysis.1 = bf16[8,512,128]{2,1,0:T(8,128)(2,1)S(1)} custom-call(s32[4,16]{1,0:T(4,128)S(1)} %copy-done.4, s32[4]{0:T(128)S(1)} %copy-done.5, bf16[8,512,128]{2,1,0:T(8,128)(2,1)S(1)} %copy-done, bf16[8,16,128]{2,1,0:T(8,128)(2,1)S(1)} %copy-done.1, f32[16,128]{1,0:T(8,128)S(1)} %copy-done.2, f32[16,128]{1,0:T(8,128)S(1)} %copy-done.3), custom_call_target="tpu_custom_call" | custom-call | tf_op jit(solution)/shard_map/analysis/pallas_call | solution.py:357
  159.2 1.0 copy.8
Async XLA Ops:
  0.0 1.2 copy-start
  1.2 0.8 copy-start.1
  2.0 0.7 copy-start.2
  2.7 0.7 copy-start.3
  3.4 0.7 copy-start.4
  4.1 0.7 copy-start.5

commit v2 on v1

--- a/solution.py
+++ b/solution.py
@@ -129,15 +129,28 @@
 
 
 def kernel(
-    lists, counts, state, obs, value, precision, out,
-    raw, vp, stage, anom, prec, inno, t_ref, f_ref, p_ref, z_ref, w_ref, cols, xb, stage2, outb,
-    rps, rpr, rms, rmr, sbs, sbr, has, har, shs, shr, vps, vpr, s1, r1, s2, r2, own,
+    lists_in, counts_in, state, obs, value, precision, out,
+    lists, counts, raw, vp, stage, anom, prec, inno, t_ref, f_ref, p_ref, z_ref, w_ref, cols, xb, stage2, outb,
+    r1s, r1r, r2s, r2r, sbs, sbr, has, har, shs, shr, vps, vpr, s1, r1, s2, r2, own,
 ):
     s, me = lax.axis_index("space"), lax.axis_index("member")
     z, c = me // 2, me % 2
-    zp, zm = ((z + 1) % NZ) * 2 + c, ((z + NZ - 1) % NZ) * 2 + c
     sibling = z * 2 + 1 - c
     up, down = (s + 1) % NSP, (s + NSP - 1) % NSP
+
+    loads = [
+        pltpu.make_async_copy(src, dst, own.at[i])
+        for i, (src, dst) in enumerate((
+            (state.at[:, pl.ds(pl.multiple_of(me * 16, 16), 16), :], cols.at[0]),
+            (lists_in, lists),
+            (counts_in, counts),
+            (obs, raw.at[1, 0]),
+            (value, vp.at[1, 0]),
+            (precision, vp.at[1, 1]),
+        ))
+    ]
+    for load in loads:
+        load.start()
 
     barrier = pltpu.get_barrier_semaphore()
     for peer in (up, down):
@@ -154,11 +167,15 @@
             src_ref=src, dst_ref=dst, send_sem=ss, recv_sem=rs, device_id=device, device_id_type=MESH
         )
 
-    def ring_up(t):
-        return rcopy(raw.at[1, 2 * ((16 - t) % 16)], raw.at[1, 2 * (15 - t)], rps.at[t], rpr.at[t], (s, zp))
-
-    def ring_down(t):
-        return rcopy(raw.at[1, 2 * t], raw.at[1, 2 * (t + 1)], rms.at[t], rmr.at[t], (s, zm))
+    def hop(side, far, k):
+        d = 2 * k + 1 + far
+        now, then = ((16 - 2 * k) % 16, 16 - d) if side == 0 else (2 * k, d)
+        sems = (r1s, r1r) if far == 0 else (r2s, r2r)
+        dz = (1 + far) if side == 0 else NZ - 1 - far
+        peer = ((z + dz) % NZ) * 2 + c
+        return rcopy(
+            raw.at[1, 2 * now], raw.at[1, 2 * then], sems[0].at[side, k], sems[1].at[side, k], (s, peer)
+        )
 
     def across(u):
         return rcopy(raw.at[1, 2 * u], raw.at[1, 2 * u + 1], sbs.at[u], sbr.at[u], (s, sibling))
@@ -210,56 +227,52 @@
             halo(side, u).wait_recv()
             halo_across(side, u).start()
 
-    own_in = pltpu.make_async_copy(state.at[:, rows_of(me), :], cols.at[0], own.at[0])
-    own_in.start()
-    raw[1, 0] = obs[...]
-    vp[1, 0] = value[...]
-    vp[1, 1] = precision[...]
-    ring_up(0).start()
-    ring_down(0).start()
+    def scatter(u):
+        send_state(u, 0).start()
+        send_state(u, 1).start()
+
+    for load in loads[3:]:
+        load.wait()
+    for side in range(2):
+        hop(side, 1, 0).start()
+    for side in range(2):
+        hop(side, 0, 0).start()
     spread(0)
     rim(0).start()
     rim(1).start()
-
-    def scatter(j):
-        u = far(j)
-        send_state(u, 0).start()
-        send_state(u, 1).start()
-
-    scatter(0)
-    scatter(1)
-
-    def step(t):
-        ring_up(t - 1).wait_recv()
-        ring_up(t).start()
-        ring_down(t - 1).wait_recv()
-
-        @pl.when(t < 7)
-        def _():
-            ring_down(t).start()
-
-        spread(16 - t)
-        spread(t)
-
-        @pl.when(t > 1)
-        def _():
-            relay(17 - t)
-            relay(t - 1)
-
-        scatter(2 * t)
-
-        @pl.when(t < 7)
-        def _():
-            scatter(2 * t + 1)
-
-    loop(1, 8, step)
+    for k in range(1, 4):
+        for side in range(2):
+            hop(side, 1, k - 1).wait_recv()
+            if k < 3 or side == 0:
+                hop(side, 1, k).start()
+        for side in range(2):
+            hop(side, 0, k).start()
+        spread(16 - 2 * k)
+        spread(2 * k)
+        for side in range(2):
+            hop(side, 0, k - 1).wait_recv()
+            spread((17 - 2 * k, 2 * k - 1)[side])
+        if k == 1:
+            relay(0)
+        else:
+            for d in (2 * k - 3, 2 * k - 2):
+                relay(16 - d)
+                relay(d)
+        scatter(k)
+        scatter(16 - k)
+    for side in range(2):
+        hop(side, 0, 3).wait_recv()
+        spread((9, 7)[side])
+    hop(0, 1, 3).wait_recv()
+    spread(8)
+    scatter(4)
+    scatter(12)
     send_state(0, 1).start()
-    ring_up(7).wait_recv()
-    spread(8)
-    relay(0)
-    relay(9)
-    relay(7)
-    relay(8)
+    for d in (5, 6, 7, 8):
+        relay(16 - d)
+        if d < 8:
+            relay(d)
+    loop(0, 7, lambda j: scatter(far(j)))
 
     def landed(u):
         across(u).wait_recv()
@@ -270,6 +283,8 @@
     rim(0).wait_recv()
     rim(1).wait_recv()
 
+    loads[1].wait()
+    loads[2].wait()
     anomalies(s, raw, vp, stage, anom, prec, inno)
     systems(lists, counts, anom, prec, inno, t_ref, f_ref)
     weights(t_ref, f_ref, p_ref, z_ref, w_ref)
@@ -278,7 +293,7 @@
         rows = cols[slot].astype(F32).reshape(128, 128)
         stage[pl.ds(pl.multiple_of(slot * 128, 128), 128), :] = rows
 
-    own_in.wait()
+    loads[0].wait()
     unpack(0)
 
     def arrive(slot):
@@ -315,7 +330,7 @@
                     send_result(u, p).start()
 
     loop(0, 4, apply)
-    own_out = pltpu.make_async_copy(outb.at[0], out.at[:, rows_of(me), :], own.at[1])
+    own_out = pltpu.make_async_copy(outb.at[0], out.at[:, rows_of(me), :], own.at[6])
     own_out.start()
 
     def settle(slot):
@@ -329,14 +344,11 @@
     loop(1, 32, settle)
     own_out.wait()
 
-    def sent(t):
-        ring_up(t).wait_send()
-
-        @pl.when(t < 7)
-        def _():
-            ring_down(t).wait_send()
-
-    loop(0, 8, sent)
+    for side in range(2):
+        for k in range(4):
+            hop(side, 0, k).wait_send()
+            if side == 0 or k < 3:
+                hop(side, 1, k).wait_send()
 
     def sent_wide(u):
         across(u).wait_send()
@@ -350,16 +362,16 @@
 
 
 def per_device(state, obs_prior, obs_value, obs_precision, block_lists, list_counts):
-    vmem = pl.BlockSpec(memory_space=pltpu.VMEM)
-    smem = pl.BlockSpec(memory_space=pltpu.SMEM)
     anywhere = pl.BlockSpec(memory_space=pl.ANY)
     dma = pltpu.SemaphoreType.DMA
     return pl.pallas_call(
         kernel,
         out_shape=jax.ShapeDtypeStruct(state.shape, state.dtype),
-        in_specs=[smem, smem, anywhere, vmem, vmem, vmem],
+        in_specs=[anywhere] * 6,
         out_specs=anywhere,
         scratch_shapes=[
+            pltpu.SMEM((NG, 16), jnp.int32),
+            pltpu.SMEM((NG,), jnp.int32),
             pltpu.VMEM((3, 32, 8, 16, 128), BF),
             pltpu.VMEM((3, 2, 16, 128), F32),
             pltpu.VMEM((4096, 128), F32),
@@ -375,12 +387,12 @@
             pltpu.VMEM((NG, MEM, 512), BF),
             pltpu.VMEM((1024, 128), F32),
             pltpu.VMEM((32, 8, 16, 128), BF),
-            dma((8,)), dma((8,)), dma((7,)), dma((7,)), dma((16,)), dma((16,)),
+            dma((2, 4)), dma((2, 4)), dma((2, 4)), dma((2, 4)), dma((16,)), dma((16,)),
             dma((2, 16)), dma((2, 16)), dma((2, 16)), dma((2, 16)), dma((2,)), dma((2,)),
-            dma((32,)), dma((32,)), dma((32,)), dma((32,)), dma((2,)),
+            dma((32,)), dma((32,)), dma((32,)), dma((32,)), dma((7,)),
         ],
         compiler_params=pltpu.CompilerParams(
-            collective_id=0, has_side_effects=True, vmem_limit_bytes=48 << 20
+            collective_id=0, has_side_effects=True, vmem_limit_bytes=62 << 20
         ),
         name="analysis",
     )(block_lists, list_counts, state, obs_prior, obs_value, obs_precision)

time: 160 us -> 128 us (0.80)
  Pallas kernels: 154 us -> 126 us
  local copies, waits for them, and re-layouts: 5.68 us -> 2.27 us
    pallas_call x1, Pallas kernels: 154 us -> 126 us  [per_device(): pl.pallas_call(kernel, out_shape=jax.ShapeDtypeStruct(state.shape, state....]
    unnamed x13 -> x1, local copies, waits for them, and re-layouts: 5.68 us -> 2.27 us
where the time goes in v2:
time: 128 us
  Pallas kernels  126 us (98%)
  local copies, waits for them, and re-layouts  2.27 us (2%)
    pallas_call x1, Pallas kernels, per_device(): pl.pallas_call(kernel, out_shape=jax.ShapeDtypeStruct(state.shape, state....  126 us

profile of v2, /device:TPU:1, one launch (start us, length us, event | category | flops | bytes accessed | tf_op | source)
XLA Modules:
  0.0 128.3 jit_solution(10244442696938384300)
XLA Ops:
  0.0 126.0 %analysis.1 = bf16[8,512,128]{2,1,0:T(8,128)(2,1)} custom-call(s32[4,16]{1,0:T(4,128)} %lists_in.1, s32[4]{0:T(128)} %counts_in.1, bf16[8,512,128]{2,1,0:T(8,128)(2,1)} %state.1, bf16[8,16,128]{2,1,0:T(8,128)(2,1)} %obs.1, f32[16,128]{1,0:T(8,128)} %value.1, f32[16,128]{1,0:T(8,128)} %precision.1), custom_call_target="tpu_custom_call" | custom-call | tf_op jit(solution)/shard_map/analysis/pallas_call | solution.py:367
  126.0 2.3 %copy.8 = bf16[8,512,128]{2,1,0:T(8,128)(2,1)} copy(bf16[8,512,128]{2,1,0:T(8,128)(2,1)} %analysis.1) | data formatting | bytes 2097152

commit v3 on v2

--- a/solution.py
+++ b/solution.py
@@ -14,6 +14,14 @@
 MEM = 256
 NZ = 16
 NSP = 16
+SCHED = (
+    ((1, 0), (2, 0)),
+    ((1, 1), (2, 1)),
+    ((3, 0), (4, 0)),
+    ((3, 1), (4, 1), (5, 0)),
+    ((6, 0), (5, 1)),
+    ((8, 0), (8, 1), (7, 0), (7, 1), (6, 1)),
+)
 
 
 def split(x):
@@ -153,14 +161,11 @@
         load.start()
 
     barrier = pltpu.get_barrier_semaphore()
-    for peer in (up, down):
-        pl.semaphore_signal(barrier, inc=1, device_id=(peer, me), device_id_type=MESH)
-
-    def greet(d):
-        pl.semaphore_signal(barrier, inc=1, device_id=(s, (me + d) % 32), device_id_type=MESH)
-
-    loop(1, 32, greet)
-    pl.semaphore_wait(barrier, 33)
+    near = [(s, ((z + d) % NZ) * 2 + c) for d in (1, 2, NZ - 2, NZ - 1)]
+    near += [(s, sibling), (up, me), (down, me)]
+    for peer in near:
+        pl.semaphore_signal(barrier, inc=1, device_id=peer, device_id_type=MESH)
+    pl.semaphore_wait(barrier, len(near))
 
     def rcopy(src, dst, ss, rs, device):
         return pltpu.make_async_remote_copy(
@@ -227,9 +232,18 @@
             halo(side, u).wait_recv()
             halo_across(side, u).start()
 
-    def scatter(u):
-        send_state(u, 0).start()
-        send_state(u, 1).start()
+    def scatter(d, p):
+        if p == 1:
+            across(d).wait_recv()
+        send_state(d, p).start()
+        if d < 8:
+            if p == 1:
+                across(16 - d).wait_recv()
+            send_state(16 - d, p).start()
+
+    def sched(i):
+        for d, p in SCHED[i]:
+            scatter(d, p)
 
     for load in loads[3:]:
         load.wait()
@@ -240,6 +254,7 @@
     spread(0)
     rim(0).start()
     rim(1).start()
+    sched(0)
     for k in range(1, 4):
         for side in range(2):
             hop(side, 1, k - 1).wait_recv()
@@ -258,24 +273,22 @@
             for d in (2 * k - 3, 2 * k - 2):
                 relay(16 - d)
                 relay(d)
-        scatter(k)
-        scatter(16 - k)
+        sched(k)
     for side in range(2):
         hop(side, 0, 3).wait_recv()
         spread((9, 7)[side])
     hop(0, 1, 3).wait_recv()
     spread(8)
-    scatter(4)
-    scatter(12)
+    sched(4)
+    across(0).wait_recv()
     send_state(0, 1).start()
     for d in (5, 6, 7, 8):
         relay(16 - d)
         if d < 8:
             relay(d)
-    loop(0, 7, lambda j: scatter(far(j)))
+    sched(5)
 
     def landed(u):
-        across(u).wait_recv()
         halo_across(0, u).wait_recv()
         halo_across(1, u).wait_recv()
 

time: 128 us -> 126 us (0.984)
  Pallas kernels: 126 us -> 124 us
    pallas_call x1, Pallas kernels: 126 us -> 124 us  [per_device(): pl.pallas_call(kernel, out_shape=jax.ShapeDtypeStruct(state.shape, state....]
where the time goes in v3:
time: 126 us
  Pallas kernels  124 us (98%)
  local copies, waits for them, and re-layouts  2.27 us (2%)
    pallas_call x1, Pallas kernels, per_device(): pl.pallas_call(kernel, out_shape=jax.ShapeDtypeStruct(state.shape, state....  124 us

profile of v3, /device:TPU:1, one launch (start us, length us, event | category | flops | bytes accessed | tf_op | source)
XLA Modules:
  0.0 126.1 jit_solution(15721071206582110861)
XLA Ops:
  0.0 123.8 %analysis.1 = bf16[8,512,128]{2,1,0:T(8,128)(2,1)} custom-call(s32[4,16]{1,0:T(4,128)} %lists_in.1, s32[4]{0:T(128)} %counts_in.1, bf16[8,512,128]{2,1,0:T(8,128)(2,1)} %state.1, bf16[8,16,128]{2,1,0:T(8,128)(2,1)} %obs.1, f32[16,128]{1,0:T(8,128)} %value.1, f32[16,128]{1,0:T(8,128)} %precision.1), custom_call_target="tpu_custom_call" | custom-call | tf_op jit(solution)/shard_map/analysis/pallas_call | solution.py:380
  123.9 2.3 %copy.8 = bf16[8,512,128]{2,1,0:T(8,128)(2,1)} copy(bf16[8,512,128]{2,1,0:T(8,128)(2,1)} %analysis.1) | data formatting | bytes 2097152

commit v4 on v3

--- a/solution.py
+++ b/solution.py
@@ -16,11 +16,11 @@
 NSP = 16
 SCHED = (
     ((1, 0), (2, 0)),
-    ((1, 1), (2, 1)),
+    ((2, 1),),
     ((3, 0), (4, 0)),
-    ((3, 1), (4, 1), (5, 0)),
+    ((4, 1), (5, 0)),
     ((6, 0), (5, 1)),
-    ((8, 0), (8, 1), (7, 0), (7, 1), (6, 1)),
+    ((8, 0), (8, 1), (7, 0), (7, 1), (6, 1), (3, 1), (1, 1)),
 )
 
 
@@ -51,33 +51,36 @@
     lax.fori_loop(low, high, step, 0)
 
 
-def anomalies(s, raw, vp, stage, anom, prec, inno):
-    for tile in range(3):
-        def add(slot, total):
-            return total + jnp.sum(raw[tile, slot].astype(F32), axis=0)
-
-        mean = lax.fori_loop(0, 32, add, jnp.zeros((16, 128), F32)) * (1.0 / MEM)
-        live = jnp.float32(1.0)
-        if tile == 0:
-            live = jnp.where(s > 0, 1.0, 0.0).astype(F32)
-        if tile == 2:
-            live = jnp.where(s < NSP - 1, 1.0, 0.0).astype(F32)
-
-        def centre(slot):
-            rows = (raw[tile, slot].astype(F32) - mean[None]) * live
-            stage[pl.ds(pl.multiple_of(slot * 128, 128), 128), :] = rows.reshape(128, 128)
-
-        loop(0, 32, centre)
-
-        def pick(b):
-            anom[tile * 16 + b] = stage[pl.ds(b, MEM, stride=16), :].astype(BF)
-
-        loop(0, 16, pick)
-        innovation = (vp[tile, 0] - mean) * live
-        precision = vp[tile, 1] * live
-        for b in range(16):
-            inno[tile * 16 + b] = innovation[b : b + 1]
-            prec[tile * 16 + b] = precision[b : b + 1]
+def anomalies(tile, raw, vp, stage, anom, prec, inno):
+    def add(slot, total):
+        return total + jnp.sum(raw[tile, slot].astype(F32), axis=0)
+
+    mean = lax.fori_loop(0, 32, add, jnp.zeros((16, 128), F32)) * (1.0 / MEM)
+
+    def centre(slot):
+        rows = raw[tile, slot].astype(F32) - mean[None]
+        stage[pl.ds(pl.multiple_of(slot * 128, 128), 128), :] = rows.reshape(128, 128)
+
+    loop(0, 32, centre)
+
+    def pick(b):
+        anom[tile * 16 + b] = stage[pl.ds(b, MEM, stride=16), :].astype(BF)
+
+    loop(0, 16, pick)
+    innovation = vp[tile, 0] - mean
+    precision = vp[tile, 1]
+    for b in range(16):
+        inno[tile * 16 + b] = innovation[b : b + 1]
+        prec[tile * 16 + b] = precision[b : b + 1]
+
+
+def no_tile(tile, anom, prec, inno):
+    def clear(b):
+        anom[tile * 16 + b] = jnp.zeros((MEM, 128), BF)
+        inno[tile * 16 + b] = jnp.zeros((1, 128), F32)
+        prec[tile * 16 + b] = jnp.zeros((1, 128), F32)
+
+    loop(0, 16, clear)
 
 
 def systems(lists, counts, anom, prec, inno, t_ref, f_ref):
@@ -145,6 +148,13 @@
     z, c = me // 2, me % 2
     sibling = z * 2 + 1 - c
     up, down = (s + 1) % NSP, (s + NSP - 1) % NSP
+    has_up, has_down = s < NSP - 1, s > 0
+
+    def toward(side, body):
+        pl.when((has_up, has_down)[side])(body)
+
+    def from_(side, body):
+        pl.when((has_down, has_up)[side])(body)
 
     loads = [
         pltpu.make_async_copy(src, dst, own.at[i])
@@ -162,10 +172,16 @@
 
     barrier = pltpu.get_barrier_semaphore()
     near = [(s, ((z + d) % NZ) * 2 + c) for d in (1, 2, NZ - 2, NZ - 1)]
-    near += [(s, sibling), (up, me), (down, me)]
+    near += [(s, sibling)]
+
+    def greet(peer):
+        pl.semaphore_signal(barrier, inc=1, device_id=peer, device_id_type=MESH)
+
     for peer in near:
-        pl.semaphore_signal(barrier, inc=1, device_id=peer, device_id_type=MESH)
-    pl.semaphore_wait(barrier, len(near))
+        greet(peer)
+    toward(0, lambda: greet((up, me)))
+    toward(1, lambda: greet((down, me)))
+    pl.semaphore_wait(barrier, len(near) + 1 + (s + NSP - 1) // NSP - (s + 1) // NSP)
 
     def rcopy(src, dst, ss, rs, device):
         return pltpu.make_async_remote_copy(
@@ -224,13 +240,17 @@
 
     def spread(u):
         across(u).start()
-        halo(0, u).start()
-        halo(1, u).start()
+        for side in range(2):
+            toward(side, lambda side=side: halo(side, u).start())
 
     def relay(u):
         for side in range(2):
-            halo(side, u).wait_recv()
-            halo_across(side, u).start()
+
+            def on(side=side):
+                halo(side, u).wait_recv()
+                halo_across(side, u).start()
+
+            from_(side, on)
 
     def scatter(d, p):
         if p == 1:
@@ -252,8 +272,8 @@
     for side in range(2):
         hop(side, 0, 0).start()
     spread(0)
-    rim(0).start()
-    rim(1).start()
+    for side in range(2):
+        toward(side, lambda side=side: rim(side).start())
     sched(0)
     for k in range(1, 4):
         for side in range(2):
@@ -288,37 +308,48 @@
             relay(d)
     sched(5)
 
-    def landed(u):
-        halo_across(0, u).wait_recv()
-        halo_across(1, u).wait_recv()
-
-    loop(0, 16, landed)
-    rim(0).wait_recv()
-    rim(1).wait_recv()
-
     loads[1].wait()
     loads[2].wait()
-    anomalies(s, raw, vp, stage, anom, prec, inno)
+    anomalies(1, raw, vp, stage, anom, prec, inno)
+    for side in range(2):
+
+        def rim_tile(side=side):
+            loop(0, 16, lambda u: halo_across(side, u).wait_recv())
+            rim(side).wait_recv()
+            anomalies(2 * side, raw, vp, stage, anom, prec, inno)
+
+        from_(side, rim_tile)
+    pl.when(s == 0)(lambda: no_tile(0, anom, prec, inno))
+    pl.when(s == NSP - 1)(lambda: no_tile(2, anom, prec, inno))
     systems(lists, counts, anom, prec, inno, t_ref, f_ref)
     weights(t_ref, f_ref, p_ref, z_ref, w_ref)
 
-    def unpack(slot):
-        rows = cols[slot].astype(F32).reshape(128, 128)
-        stage[pl.ds(pl.multiple_of(slot * 128, 128), 128), :] = rows
-
-    loads[0].wait()
-    unpack(0)
-
-    def arrive(slot):
+    def unpack(u):
+        for p in range(2):
+            rows = cols[2 * u + p].astype(F32).reshape(128, 128)
+            stage[pl.ds(pl.multiple_of(u * 256 + p * 128, 128), 128), :] = rows
+        members = pl.ds(pl.multiple_of(u * 16, 16), 16)
+        for g in range(NG):
+            for r in range(4):
+                rows = stage[pl.ds(u * 256 + 4 * g + r, 16, stride=16), :]
+                xb[g, members, r * 128 : (r + 1) * 128] = rows.astype(BF)
+
+    def await_state(slot):
         rcopy(
             state.at[:, pl.ds(0, 16), :], cols.at[slot], s1.at[slot], r1.at[slot], (s, sibling)
         ).wait_recv()
-        unpack(slot)
-
-    loop(1, 32, arrive)
-    for g in range(NG):
-        for r in range(4):
-            xb[g, :, r * 128 : (r + 1) * 128] = stage[pl.ds(4 * g + r, MEM, stride=16), :].astype(BF)
+
+    loads[0].wait()
+    await_state(1)
+    unpack(0)
+
+    def arrive(j):
+        u = far(14 - j)
+        await_state(2 * u)
+        await_state(2 * u + 1)
+        unpack(u)
+
+    loop(0, 15, arrive)
 
     def apply(part):
         far_of = [far(4 * part + i) for i in range(4)]
@@ -366,12 +397,12 @@
     def sent_wide(u):
         across(u).wait_send()
         for side in range(2):
-            halo(side, u).wait_send()
-            halo_across(side, u).wait_send()
+            toward(side, lambda side=side: halo(side, u).wait_send())
+            from_(side, lambda side=side: halo_across(side, u).wait_send())
 
     loop(0, 16, sent_wide)
-    rim(0).wait_send()
-    rim(1).wait_send()
+    for side in range(2):
+        toward(side, lambda side=side: rim(side).wait_send())
 
 
 def per_device(state, obs_prior, obs_value, obs_precision, block_lists, list_counts):
@@ -380,7 +411,7 @@
     return pl.pallas_call(
         kernel,
         out_shape=jax.ShapeDtypeStruct(state.shape, state.dtype),
-        in_specs=[anywhere] * 6,
+        in_specs=[pl.BlockSpec(memory_space=pltpu.HBM)] * 6,
         out_specs=anywhere,
         scratch_shapes=[
             pltpu.SMEM((NG, 16), jnp.int32),

time: 126 us -> 121 us (0.960); the launches traced: 126 us -> 119 us
  Pallas kernels: 124 us -> 116 us
    pallas_call x1, Pallas kernels: 124 us -> 116 us  [per_device(): pl.pallas_call(kernel, out_shape=jax.ShapeDtypeStruct(state.shape, state....]
where the time goes in v4:
time: 121 us; the launch traced here: 119 us
  Pallas kernels  116 us (96%)
  local copies, waits for them, and re-layouts  2.27 us (2%)
    pallas_call x1, Pallas kernels, per_device(): pl.pallas_call(kernel, out_shape=jax.ShapeDtypeStruct(state.shape, state....  116 us

profile of v4, /device:TPU:1, one launch (start us, length us, event | category | flops | bytes accessed | tf_op | source)
XLA Modules:
  0.0 118.8 jit_solution(17261140366737323949)
XLA Ops:
  0.0 116.5 %analysis.1 = bf16[8,512,128]{2,1,0:T(8,128)(2,1)} custom-call(s32[4,16]{1,0:T(4,128)} %lists_in.1, s32[4]{0:T(128)} %counts_in.1, bf16[8,512,128]{2,1,0:T(8,128)(2,1)} %state.1, bf16[8,16,128]{2,1,0:T(8,128)(2,1)} %obs.1, f32[16,128]{1,0:T(8,128)} %value.1, f32[16,128]{1,0:T(8,128)} %precision.1), custom_call_target="tpu_custom_call" | custom-call | tf_op jit(solution)/shard_map/analysis/pallas_call | solution.py:411
  116.5 2.3 %copy.8 = bf16[8,512,128]{2,1,0:T(8,128)(2,1)} copy(bf16[8,512,128]{2,1,0:T(8,128)(2,1)} %analysis.1) | data formatting | bytes 2097152

commit v5 on v4

--- a/solution.py
+++ b/solution.py
@@ -20,7 +20,10 @@
     ((3, 0), (4, 0)),
     ((4, 1), (5, 0)),
     ((6, 0), (5, 1)),
-    ((8, 0), (8, 1), (7, 0), (7, 1), (6, 1), (3, 1), (1, 1)),
+)
+REST = (
+    ((8, 0), (7, 0), (8, 1), (7, 1), (6, 1), (3, 1), (1, 1)),
+    ((8, 1), (7, 1), (6, 1), (3, 1), (1, 1), (8, 0), (7, 0)),
 )
 
 
@@ -86,57 +89,67 @@
 def systems(lists, counts, anom, prec, inno, t_ref, f_ref):
     def group(g):
         count = counts[g]
-        total = jnp.zeros((MEM + 16, MEM), F32)
-        for pair in range(8):
-            ys, ss, ws = [], [], []
-            for e in (2 * pair, 2 * pair + 1):
-                b = lists[g, e]
-                y = anom[b]
-                r = prec[b] * jnp.where(e < count, 1.0, 0.0).astype(F32)
-                ys.append(y)
-                ss.append((y.astype(F32) * r).astype(BF))
-                ws.append(jnp.broadcast_to((r * inno[b]).astype(BF), (16, 128)))
-            left = jnp.concatenate([jnp.concatenate(ss, 1), jnp.concatenate(ws, 1)], 0)
-            total = total + lax.dot_general(
-                left, jnp.concatenate(ys, 1), (((1,), (1,)), ((), ())), preferred_element_type=F32
-            )
+        ys, ss, ws = [], [], []
+        for e in range(16):
+            b = lists[g, e]
+            y = anom[b]
+            r = prec[b] * jnp.where(e < count, 1.0, 0.0).astype(F32)
+            ys.append(y)
+            ss.append((y.astype(F32) * r).astype(BF))
+            ws.append(jnp.broadcast_to((r * inno[b]).astype(BF), (16, 128)))
+        left = jnp.concatenate([jnp.concatenate(ss, 1), jnp.concatenate(ws, 1)], 0)
+        total = lax.dot_general(
+            left, jnp.concatenate(ys, 1), (((1,), (1,)), ((), ())), preferred_element_type=F32
+        )
         t_ref[g] = total[:MEM] + (MEM - 1.0) * eye()
         f_ref[g] = total[MEM:]
 
-    loop(0, NG, group)
+    def two(i):
+        group(2 * i)
+        group(2 * i + 1)
+
+    loop(0, NG // 2, two)
 
 
 def weights(t_ref, f_ref, p_ref, z_ref, w_ref):
-    def first(g):
-        t = t_ref[g]
-        norm = jnp.sqrt(jnp.sum(t * t, keepdims=True))
-        iterate = t / norm
-        factor = split(1.5 * eye() - 0.5 * iterate)
-        z_ref[g, 0], z_ref[g, 1] = factor
-        p_ref[g, 0], p_ref[g, 1] = split(dot3(split(iterate), factor))
-        t_ref[g, 0:8, 0:128] = jnp.broadcast_to(norm, (8, 128))
-
-    loop(0, NG, first)
-
-    def sweep(step):
-        g = lax.rem(step, NG)
-        z = z_ref[g, 0], z_ref[g, 1]
-        p = p_ref[g, 0], p_ref[g, 1]
-        factor = split(1.5 * eye() - 0.5 * dot3(z, p))
-        p_ref[g, 0], p_ref[g, 1] = split(dot3(p, factor))
-        z_ref[g, 0], z_ref[g, 1] = split(dot3(factor, z))
-
-    loop(0, (NS_ITERS - 1) * NG, sweep)
-
-    def last(g):
-        z = z_ref[g, 0], z_ref[g, 1]
-        norm = t_ref[g, 0:1, 0:1]
-        mean = dot3(split(dot3(split(f_ref[g]), z)), z)[0:1] / norm
-        w = (z[0].astype(F32) + z[1].astype(F32)) * (math.sqrt(MEM - 1.0) / jnp.sqrt(norm)) + mean
+    groups = range(NG)
+
+    def load(ref):
+        return [(ref[g, 0], ref[g, 1]) for g in groups]
+
+    def store(ref, values):
+        for g in groups:
+            ref[g, 0], ref[g, 1] = split(values[g])
+
+    systems_ = [t_ref[g] for g in groups]
+    norms = [jnp.sqrt(jnp.sum(t * t, keepdims=True)) for t in systems_]
+    iterates = [t / norm for t, norm in zip(systems_, norms)]
+    factors = [1.5 * eye() - 0.5 * iterate for iterate in iterates]
+    store(p_ref, [dot3(split(p), split(f)) for p, f in zip(iterates, factors)])
+    store(z_ref, factors)
+
+    def sweep(final):
+        zs, ps = load(z_ref), load(p_ref)
+        products = [dot3(z, p) for z, p in zip(zs, ps)]
+        factors = [split(1.5 * eye() - 0.5 * product) for product in products]
+        if not final:
+            next_p = [dot3(p, f) for p, f in zip(ps, factors)]
+        next_z = [dot3(f, z) for f, z in zip(factors, zs)]
+        if not final:
+            store(p_ref, next_p)
+        store(z_ref, next_z)
+
+    loop(0, NS_ITERS - 2, lambda i: sweep(False))
+    sweep(True)
+
+    zs = load(z_ref)
+    halves = [split(dot3(split(f_ref[g]), zs[g])) for g in groups]
+    means = [dot3(halves[g], zs[g])[0:1] / norms[g] for g in groups]
+    for g in groups:
+        high, low = zs[g]
+        w = (high.astype(F32) + low.astype(F32)) * (math.sqrt(MEM - 1.0) / jnp.sqrt(norms[g])) + means[g]
         w = w + (1.0 - jnp.sum(w, axis=1, keepdims=True)) * (1.0 / MEM)
         w_ref[g, 0], w_ref[g, 1] = split(w)
-
-    loop(0, NG, last)
 
 
 def kernel(
@@ -306,7 +319,13 @@
         relay(16 - d)
         if d < 8:
             relay(d)
-    sched(5)
+    for core in range(2):
+
+        def rest(core=core):
+            for d, p in REST[core]:
+                scatter(d, p)
+
+        pl.when(c == core)(rest)
 
     loads[1].wait()
     loads[2].wait()

time: 121 us -> 118 us (0.975); the launches traced: 119 us -> 118 us
  no operation moved by 1% of the time
where the time goes in v5:
time: 118 us
  Pallas kernels  115 us (97%)
  local copies, waits for them, and re-layouts  2.27 us (2%)
    pallas_call x1, Pallas kernels, per_device(): pl.pallas_call(kernel, out_shape=jax.ShapeDtypeStruct(state.shape, state....  115 us

profile of v5, /device:TPU:1, one launch (start us, length us, event | category | flops | bytes accessed | tf_op | source)
XLA Modules:
  0.0 117.7 jit_solution(2735797169560676828)
XLA Ops:
  0.0 115.4 %analysis.1 = bf16[8,512,128]{2,1,0:T(8,128)(2,1)} custom-call(s32[4,16]{1,0:T(4,128)} %lists_in.1, s32[4]{0:T(128)} %counts_in.1, bf16[8,512,128]{2,1,0:T(8,128)(2,1)} %state.1, bf16[8,16,128]{2,1,0:T(8,128)(2,1)} %obs.1, f32[16,128]{1,0:T(8,128)} %value.1, f32[16,128]{1,0:T(8,128)} %precision.1), custom_call_target="tpu_custom_call" | custom-call | tf_op jit(solution)/shard_map/analysis/pallas_call | solution.py:430
  115.4 2.3 %copy.8 = bf16[8,512,128]{2,1,0:T(8,128)(2,1)} copy(bf16[8,512,128]{2,1,0:T(8,128)(2,1)} %analysis.1) | data formatting | bytes 2097152

commit v6 on v5

--- a/solution.py
+++ b/solution.py
@@ -169,6 +169,18 @@
     def from_(side, body):
         pl.when((has_down, has_up)[side])(body)
 
+    barrier = pltpu.get_barrier_semaphore()
+    near = [(s, ((z + d) % NZ) * 2 + c) for d in (1, 2, NZ - 2, NZ - 1)]
+    near += [(s, sibling)]
+
+    def greet(peer):
+        pl.semaphore_signal(barrier, inc=1, device_id=peer, device_id_type=MESH)
+
+    for peer in near:
+        greet(peer)
+    toward(0, lambda: greet((up, me)))
+    toward(1, lambda: greet((down, me)))
+
     loads = [
         pltpu.make_async_copy(src, dst, own.at[i])
         for i, (src, dst) in enumerate((
@@ -182,18 +194,6 @@
     ]
     for load in loads:
         load.start()
-
-    barrier = pltpu.get_barrier_semaphore()
-    near = [(s, ((z + d) % NZ) * 2 + c) for d in (1, 2, NZ - 2, NZ - 1)]
-    near += [(s, sibling)]
-
-    def greet(peer):
-        pl.semaphore_signal(barrier, inc=1, device_id=peer, device_id_type=MESH)
-
-    for peer in near:
-        greet(peer)
-    toward(0, lambda: greet((up, me)))
-    toward(1, lambda: greet((down, me)))
     pl.semaphore_wait(barrier, len(near) + 1 + (s + NSP - 1) // NSP - (s + 1) // NSP)
 
     def rcopy(src, dst, ss, rs, device):
@@ -278,13 +278,14 @@
         for d, p in SCHED[i]:
             scatter(d, p)
 
-    for load in loads[3:]:
-        load.wait()
+    loads[3].wait()
     for side in range(2):
         hop(side, 1, 0).start()
     for side in range(2):
         hop(side, 0, 0).start()
     spread(0)
+    loads[4].wait()
+    loads[5].wait()
     for side in range(2):
         toward(side, lambda side=side: rim(side).start())
     sched(0)

time: 118 us -> 118 us (level)
  no operation moved by 1% of the time
where the time goes in v6:
time: 118 us
  Pallas kernels  115 us (97%)
  local copies, waits for them, and re-layouts  2.27 us (2%)
    pallas_call x1, Pallas kernels, per_device(): pl.pallas_call(kernel, out_shape=jax.ShapeDtypeStruct(state.shape, state....  115 us

profile of v6, /device:TPU:1, one launch (start us, length us, event | category | flops | bytes accessed | tf_op | source)
XLA Modules:
  0.0 117.7 jit_solution(8232427891834083089)
XLA Ops:
  0.0 115.4 %analysis.1 = bf16[8,512,128]{2,1,0:T(8,128)(2,1)} custom-call(s32[4,16]{1,0:T(4,128)} %lists_in.1, s32[4]{0:T(128)} %counts_in.1, bf16[8,512,128]{2,1,0:T(8,128)(2,1)} %state.1, bf16[8,16,128]{2,1,0:T(8,128)(2,1)} %obs.1, f32[16,128]{1,0:T(8,128)} %value.1, f32[16,128]{1,0:T(8,128)} %precision.1), custom_call_target="tpu_custom_call" | custom-call | tf_op jit(solution)/shard_map/analysis/pallas_call | solution.py:431
  115.4 2.3 %copy.8 = bf16[8,512,128]{2,1,0:T(8,128)(2,1)} copy(bf16[8,512,128]{2,1,0:T(8,128)(2,1)} %analysis.1) | data formatting | bytes 2097152

commit v7 on v6

--- a/solution.py
+++ b/solution.py
@@ -438,7 +438,7 @@
             pltpu.SMEM((NG,), jnp.int32),
             pltpu.VMEM((3, 32, 8, 16, 128), BF),
             pltpu.VMEM((3, 2, 16, 128), F32),
-            pltpu.VMEM((4096, 128), F32),
+            pltpu.VMEM((4096 + 16, 128), F32),
             pltpu.VMEM((48, MEM, 128), BF),
             pltpu.VMEM((48, 1, 128), F32),
             pltpu.VMEM((48, 1, 128), F32),
@@ -449,7 +449,7 @@
             pltpu.VMEM((NG, 2, MEM, MEM), BF),
             pltpu.VMEM((32, 8, 16, 128), BF),
             pltpu.VMEM((NG, MEM, 512), BF),
-            pltpu.VMEM((1024, 128), F32),
+            pltpu.VMEM((1024 + 16, 128), F32),
             pltpu.VMEM((32, 8, 16, 128), BF),
             dma((2, 4)), dma((2, 4)), dma((2, 4)), dma((2, 4)), dma((16,)), dma((16,)),
             dma((2, 16)), dma((2, 16)), dma((2, 16)), dma((2, 16)), dma((2,)), dma((2,)),

time: 118 us -> 118 us (level)
  no operation moved by 1% of the time
where the time goes in v7:
time: 118 us
  Pallas kernels  115 us (97%)
  local copies, waits for them, and re-layouts  2.27 us (2%)
    pallas_call x1, Pallas kernels, per_device(): pl.pallas_call(kernel, out_shape=jax.ShapeDtypeStruct(state.shape, state....  115 us

profile of v7, /device:TPU:1, one launch (start us, length us, event | category | flops | bytes accessed | tf_op | source)
XLA Modules:
  0.0 117.7 jit_solution(4928222945780526525)
XLA Ops:
  0.0 115.4 %analysis.1 = bf16[8,512,128]{2,1,0:T(8,128)(2,1)} custom-call(s32[4,16]{1,0:T(4,128)} %lists_in.1, s32[4]{0:T(128)} %counts_in.1, bf16[8,512,128]{2,1,0:T(8,128)(2,1)} %state.1, bf16[8,16,128]{2,1,0:T(8,128)(2,1)} %obs.1, f32[16,128]{1,0:T(8,128)} %value.1, f32[16,128]{1,0:T(8,128)} %precision.1), custom_call_target="tpu_custom_call" | custom-call | tf_op jit(solution)/shard_map/analysis/pallas_call | solution.py:431
  115.4 2.3 %copy.8 = bf16[8,512,128]{2,1,0:T(8,128)(2,1)} copy(bf16[8,512,128]{2,1,0:T(8,128)(2,1)} %analysis.1) | data formatting | bytes 2097152
